TPU v7x, 128 devices: a whole 4x4x4 slice. The times are simulated.
128 devices in a mesh: hi: 4 (over x_lo, core), lo: 32 (over z, x_hi, y).
Axes of the slice: x: 4 (x_hi: 2, x_lo: 2; x = x_hi * 2 + x_lo), y: 4, z: 4, core: 2. Of those that a mesh axis runs over, the one named last changes fastest.
Arguments:
- coefficients: bfloat16 [32768, 16, 128], P(('hi', 'lo')), may hold values from -6 to 6
- interpolation: bfloat16 [8, 2, 64, 64], replicated, may hold values from -0.5 to 0.5
- phases: float32 [8, 32768, 192], P(None, ('hi', 'lo')), may hold values from -3.140625 to 3.140625
Outputs:
- ordered: bfloat16 [32768, 16, 128], P(('hi', 'lo'))
All inputs are finite; a program needn't handle non-finite values.
Results may differ from a plain program's by a relative error of at most 0.025.
Values may be sent and summed in bfloat16 or wider, within the bound.
A program may use at most 192 MiB of HBM per device.

v0:
```python
import functools

import jax
import jax.numpy as jnp
from jax import lax
from jax.experimental import pallas as pl
from jax.experimental.pallas import tpu as pltpu
from jax.sharding import PartitionSpec as P

MESH = pl.DeviceIdType.MESH
BF16, F32 = jnp.bfloat16, jnp.float32
DEVICES = 128
LOWER = 32
LEVELS = 8
KINDS = 16
SCALE = 240.0

SIN = (6.28305505, -41.3311661, 81.3660033, -74.4730454, 32.7714685)
COS = (0.999999216, -19.7389812, 64.9286774, -85.2717657, 58.7907877, -21.0709971)


def reverse7(i):
    total = 0
    for bit in range(7):
        total = total + lax.rem(lax.div(i, 2**bit), 2) * 2 ** (6 - bit)
    return total


def wrap(turns):
    return turns - jnp.round(turns)


def encode(turns):
    return jnp.exp2(turns * SCALE)


def decode(code):
    return jnp.log2(code.astype(F32)) * (1.0 / SCALE)


def poly(coefs, square):
    value = jnp.full_like(square, coefs[-1])
    for c in coefs[-2::-1]:
        value = value * square + c
    return value


def tables(turns):
    square = turns * turns
    sine, cosine = poly(SIN, square) * turns, poly(COS, square)
    first = lax.broadcasted_iota(jnp.int32, turns.shape, 1) < 64
    sine_r, cosine_r = pltpu.roll(sine, 64, 1), pltpu.roll(cosine, 64, 1)
    return (
        (jnp.where(first, cosine, cosine_r), jnp.where(first, -sine, sine_r)),
        (jnp.where(first, cosine_r, cosine), jnp.where(first, -sine_r, sine)),
    )


def kernel(
    coef_hbm, interp_hbm, phase_hbm, out_ref,
    xin, phin, win, weights, a_cos, a_sin, ex_send, ex_recv, b_turns, stage,
    ph_send, ph_recv, co_send, co_recv, t_cos, t_sin, xs, ms,
    in_sem, ex_ssem, ex_rsem, ph_ssem, ph_rsem, co_ssem, co_rsem,
):
    hi, lo = lax.axis_index("hi"), lax.axis_index("lo")
    me = hi * LOWER + lo
    my_slot = reverse7(me)

    def place(d):
        return (lax.div(d, LOWER), lax.rem(d, LOWER))

    def others(f):
        def step(k, carry):
            f(lax.rem(me + k, DEVICES))
            return carry

        lax.fori_loop(1, DEVICES, step, 0)

    barrier = pltpu.get_barrier_semaphore()
    others(
        lambda d: pl.semaphore_signal(barrier, inc=1, device_id=place(d), device_id_type=MESH)
    )
    loads = [
        pltpu.make_async_copy(src, dst, in_sem.at[i])
        for i, (src, dst) in enumerate(((phase_hbm, phin), (coef_hbm, xin), (interp_hbm, win)))
    ]
    for load in loads:
        load.start()

    loads[0].wait()

    def angles(jb, carry):
        j0 = jb * 16
        rows0, rows1 = pl.ds(j0, 16), pl.ds(128 + j0, 16)

        def put(kind, turns):
            stage[pl.ds(j0 * KINDS + kind, 16, stride=KINDS), :] = encode(turns)

        c_before = None
        for l in range(LEVELS):
            t0, t1 = phin[l, rows0, 0:128], phin[l, rows1, 0:128]
            inverse = 0.15915494309189535
            t0, t1 = t0 * inverse, t1 * inverse
            first = lax.broadcasted_iota(jnp.int32, t0.shape, 1) < 64
            a = jnp.where(first, t0, pltpu.roll(t1, 64, 1))
            b = jnp.where(first, pltpu.roll(t0, 64, 1), t1)
            c = jnp.concatenate([phin[l, rows0, 128:192], phin[l, rows1, 128:192]], axis=1)
            c = c * inverse
            if l == 0:
                ex_send[0, rows0, :] = encode(a).astype(BF16)
                pairs = tables(a)
                for q in range(2):
                    a_cos[q, rows0, :], a_sin[q, rows0, :] = pairs[q]
            else:
                put(2 * l - 1, wrap(c_before + a))
            if l < 7:
                b_turns[l, rows0, :] = b
            else:
                put(14, wrap(pltpu.roll(c_before, 64, 1) + b))
                put(15, c)
            if l < 6:
                ex_send[l + 1, rows0, :] = encode(c).astype(BF16)
            c_before = c
        return carry

    lax.fori_loop(0, 8, angles, 0)

    loads[1].wait()

    def turn(j, carry):
        d = reverse7(j)
        for q in range(2):
            x = xin[q * 128 + j].astype(F32)
            cosine = jnp.broadcast_to(a_cos[q, pl.ds(j, 1), :], x.shape)
            sine = jnp.broadcast_to(a_sin[q, pl.ds(j, 1), :], x.shape)
            y = (x * cosine + pltpu.roll(x, 64, 1) * sine).astype(BF16)
            for h in range(2):
                co_send[2 * h + q, d] = y[8 * h : 8 * h + 8]
        return carry

    lax.fori_loop(0, 128, turn, 0, unroll=4)

    loads[2].wait()
    for l in range(LEVELS):
        empty = jnp.zeros((64, 64), F32)
        for part in range(2):
            block = win[l, part].astype(F32)
            row = part * 128
            weights[l, row : row + 64, :] = jnp.concatenate(
                [block, empty, empty, block], axis=1
            ).astype(BF16)
            weights[l, row + 64 : row + 128, :] = jnp.concatenate(
                [empty, block, block, empty], axis=1
            ).astype(BF16)

    pl.semaphore_wait(barrier, DEVICES - 1)

    exchanges = []
    for l in range(7):
        bit = 2 ** (6 - l)
        partner = me + bit * (1 - 2 * lax.rem(lax.div(me, bit), 2))
        exchanges.append(
            pltpu.make_async_remote_copy(
                src_ref=ex_send.at[l], dst_ref=ex_recv.at[l],
                send_sem=ex_ssem.at[l], recv_sem=ex_rsem.at[l],
                device_id=place(partner), device_id_type=MESH,
            )
        )
        exchanges[-1].start()

    def send_coefs(c):
        others(
            lambda d: pltpu.make_async_remote_copy(
                src_ref=co_send.at[c, d], dst_ref=co_recv.at[c, my_slot],
                send_sem=co_ssem.at[c], recv_sem=co_rsem.at[c],
                device_id=place(d), device_id_type=MESH,
            ).start()
        )
        co_recv[c, my_slot] = co_send[c, me]

    send_coefs(0)

    for l in range(7):
        exchanges[l].wait_recv()

    def crossed(jb, carry):
        j0 = jb * 16
        rows = pl.ds(j0, 16)
        for l in range(7):
            theirs, mine = decode(ex_recv[l, rows, :]), b_turns[l, rows, :]
            turns = wrap(mine - theirs) if l == 0 else wrap(mine + theirs)
            stage[pl.ds(j0 * KINDS + 2 * l, 16, stride=KINDS), :] = encode(turns)
        return carry

    lax.fori_loop(0, 8, crossed, 0)

    def pack(j, carry):
        ph_send[reverse7(j)] = stage[pl.ds(j * KINDS, KINDS), :].astype(BF16)
        return carry

    lax.fori_loop(0, 128, pack, 0, unroll=4)

    others(
        lambda d: pltpu.make_async_remote_copy(
            src_ref=ph_send.at[d], dst_ref=ph_recv.at[my_slot],
            send_sem=ph_ssem, recv_sem=ph_rsem,
            device_id=place(d), device_id_type=MESH,
        ).start()
    )
    ph_recv[my_slot] = ph_send[me]
    for c in range(1, 4):
        send_coefs(c)

    all_but_one = pl.ds(0, DEVICES - 1)
    pltpu.make_async_copy(ph_send.at[all_but_one], ph_recv.at[all_but_one], ph_rsem).wait()

    def make_tables(t, carry):
        pairs = tables(decode(ph_recv[t]))
        for q in range(2):
            rows = pl.ds(t * KINDS, KINDS)
            t_cos[q, rows, :], t_sin[q, rows, :] = pairs[q]
        return carry

    lax.fori_loop(0, 128, make_tables, 0, unroll=4)

    def table(q, t, kind):
        row = pl.ds(t * KINDS + kind, 1)
        return (
            jnp.broadcast_to(t_cos[q, row, :], (8, 128)),
            jnp.broadcast_to(t_sin[q, row, :], (8, 128)),
        )

    def state(q, t):
        rows = pl.ds(pl.multiple_of(t * 8, 8), 8)
        return ms[q, rows, 0:128], ms[q, rows, 128:256]

    def turned(planes, angle):
        return planes[0] * angle[0] + planes[1] * angle[1]

    def put_unit(q, unit, columns, values):
        rows = pl.ds(pl.multiple_of(unit * 16, 16), 16)
        xs[q, rows, columns] = jnp.concatenate(values, axis=0).astype(BF16)

    own, cross = slice(0, 128), slice(128, 256)

    def multiply(q, l):
        for part in range(4):
            rows = slice(256 * part, 256 * part + 256)
            ms[q, rows, :] = jnp.dot(xs[q, rows, :], weights[l], preferred_element_type=F32)

    def levels(h, q):
        c = 2 * h + q
        pltpu.make_async_copy(
            co_send.at[c, all_but_one], co_recv.at[c, all_but_one], co_rsem.at[c]
        ).wait()

        def first_level(unit, carry):
            t = 2 * unit
            y = [co_recv[c, t + i].astype(F32) for i in range(2)]
            put_unit(q, unit, own, y)
            planes = [(v, pltpu.roll(v, 64, 1)) for v in y]
            put_unit(
                q, unit, cross, [turned(planes[1 - i], table(q, t + i, 0)) for i in range(2)]
            )
            return carry

        lax.fori_loop(0, 64, first_level, 0, unroll=4)
        multiply(q, 0)
        for l in range(1, 7):
            stride = 2 ** (l - 1)

            def one_pair(pair, carry, l=l, stride=stride):
                u0 = lax.div(pair, stride) * (2 * stride) + lax.rem(pair, stride)
                units = (u0, u0 + stride)
                planes = [[state(q, 2 * u + i) for i in range(2)] for u in units]
                for k in range(2):
                    u = units[k]
                    put_unit(
                        q, u, own,
                        [turned(planes[k][i], table(q, 2 * u + i, 2 * l - 1)) for i in range(2)],
                    )
                    put_unit(
                        q, u, cross,
                        [turned(planes[1 - k][i], table(q, 2 * u + i, 2 * l)) for i in range(2)],
                    )
                return carry

            lax.fori_loop(0, 32, one_pair, 0, unroll=4)
            multiply(q, l)

    def half(h, carry):
        def part(q, carry):
            levels(h, q)
            return carry

        lax.fori_loop(0, 2, part, 0)

        def last_level(unit, carry):
            planes = [[state(q, 2 * unit + i) for i in range(2)] for q in range(2)]
            for q in range(2):
                put_unit(
                    q, unit, own,
                    [turned(planes[q][i], table(q, 2 * unit + i, 13)) for i in range(2)],
                )
                put_unit(
                    q, unit, cross,
                    [turned(planes[1 - q][i], table(q, 2 * unit + i, 14)) for i in range(2)],
                )
            return carry

        lax.fori_loop(0, 64, last_level, 0, unroll=4)
        for q in range(2):
            multiply(q, 7)

            def finish(t, carry, q=q):
                result = turned(state(q, t), table(q, t, 15)).astype(BF16)
                out_ref[q * 128 + t, pl.ds(pl.multiple_of(8 * h, 8), 8), :] = result
                return carry

            lax.fori_loop(0, 128, finish, 0, unroll=8)
        return carry

    lax.fori_loop(0, 2, half, 0)

    for l in range(7):
        exchanges[l].wait_send()
    pltpu.make_async_copy(ph_send.at[all_but_one], ph_recv.at[all_but_one], ph_ssem).wait()
    for c in range(4):
        pltpu.make_async_copy(
            co_send.at[c, all_but_one], co_recv.at[c, all_but_one], co_ssem.at[c]
        ).wait()


def body(coefficients, interpolation, phases):
    vmem, dma = pltpu.VMEM, pltpu.SemaphoreType.DMA
    return pl.pallas_call(
        kernel,
        out_shape=jax.ShapeDtypeStruct(coefficients.shape, BF16),
        in_specs=[pl.BlockSpec(memory_space=pl.ANY)] * 3,
        out_specs=pl.BlockSpec(memory_space=pltpu.VMEM),
        scratch_shapes=[
            vmem((256, 16, 128), BF16),
            vmem((LEVELS, 256, 192), F32),
            vmem((LEVELS, 2, 64, 64), BF16),
            vmem((LEVELS, 256, 256), BF16),
            vmem((2, 128, 128), F32),
            vmem((2, 128, 128), F32),
            vmem((7, 128, 128), BF16),
            vmem((7, 128, 128), BF16),
            vmem((7, 128, 128), F32),
            vmem((128 * KINDS, 128), F32),
            vmem((128, KINDS, 128), BF16),
            vmem((128, KINDS, 128), BF16),
            vmem((4, 128, 8, 128), BF16),
            vmem((4, 128, 8, 128), BF16),
            vmem((2, 128 * KINDS, 128), F32),
            vmem((2, 128 * KINDS, 128), F32),
            vmem((2, 1024, 256), BF16),
            vmem((2, 1024, 256), F32),
            dma((3,)),
            dma((7,)),
            dma((7,)),
            dma,
            dma,
            dma((4,)),
            dma((4,)),
        ],
        compiler_params=pltpu.CompilerParams(
            collective_id=0, has_side_effects=True, vmem_limit_bytes=40 * 2**20
        ),
    )(coefficients, interpolation, phases)


def solution(mesh):
    placed = (P(("hi", "lo"), None, None), P(), P(None, ("hi", "lo"), None))
    return jax.shard_map(
        body, mesh=mesh, in_specs=placed, out_specs=P(("hi", "lo"), None, None), check_vma=False
    )
```

profile of v0, /device:TPU:1, one launch (start us, length us, event | category | flops | bytes accessed | tf_op | source)
XLA Modules:
  0.0 63.0 jit_solution(4980397382952868575)
XLA Ops:
  0.0 0.0 copy-start.1
  0.0 0.0 copy-start
  0.0 1.9 %copy.4.phase_hbm = f32[8,256,192]{2,1,0:T(8,128)S(1)} copy(f32[8,256,192]{1,2,0:T(8,128)} %param.5) | data formatting | bytes 3145728 | tf_op args[2]
  1.9 0.0 copy-done.1
  2.0 0.0 copy-done
  2.0 60.1 %shard_map.37 = bf16[256,16,128]{2,1,0:T(8,128)(2,1)S(1)} custom-call(bf16[256,16,128]{2,1,0:T(8,128)(2,1)S(1)} %copy-done, bf16[8,2,64,64]{3,2,1,0:T(8,128)(2,1)S(1)} %copy-done.1, f32[8,256,192]{2,1,0:T(8,128)S(1)} %copy.4.phase_hbm), custom_call_target="tpu_custom_call" | custom-call | tf_op jit(solution)/shard_map/pallas_call | solution.py:336
  62.0 1.0 %copy.6 = bf16[256,16,128]{2,1,0:T(8,128)(2,1)} copy(bf16[256,16,128]{2,1,0:T(8,128)(2,1)S(1)} %shard_map.37) | data formatting | bytes 2097152
Async XLA Ops:
  0.0 1.9 %copy-start.1 = (bf16[8,2,64,64]{3,2,1,0:T(8,128)(2,1)S(1)}, bf16[8,2,64,64]{3,2,1,0:T(8,128)(2,1)}, u32[]{:S(2)}) copy-start(bf16[8,2,64,64]{3,2,1,0:T(8,128)(2,1)} %interp_hbm.1) | copy-start | bytes 393220
  0.0 2.0 %copy-start = (bf16[256,16,128]{2,1,0:T(8,128)(2,1)S(1)}, bf16[256,16,128]{2,1,0:T(8,128)(2,1)}, u32[]{:S(2)}) copy-start(bf16[256,16,128]{2,1,0:T(8,128)(2,1)} %coef_hbm.1) | copy-start | bytes 3145732
where the time goes:
time: 64 us; the launch traced here: 63 us
  Pallas kernels  60.1 us (94%)
  local copies, waits for them, and re-layouts  2.91 us (5%)
    pallas_call x1, Pallas kernels, body(): pl.pallas_call(kernel, out_shape=jax.ShapeDtypeStruct(coefficients.shape,...  60.1 us
    unnamed x6, local copies, waits for them, and re-layouts  2.91 us

commit v1 on v0

v1 whole, which is shorter than its diff:
```python
import functools

import jax
import jax.numpy as jnp
from jax import lax
from jax.experimental import pallas as pl
from jax.experimental.pallas import tpu as pltpu
from jax.sharding import PartitionSpec as P

MESH = pl.DeviceIdType.MESH
BF16, F32 = jnp.bfloat16, jnp.float32
DEVICES = 128
LOWER = 32
LEVELS = 8
GROUPS = 3
SCALE = 240.0

SIN = (6.28305505, -41.3311661, 81.3660033, -74.4730454, 32.7714685)
COS = (0.999999216, -19.7389812, 64.9286774, -85.2717657, 58.7907877, -21.0709971)


def reverse7(i):
    total = 0
    for bit in range(7):
        total = total + lax.rem(lax.div(i, 2**bit), 2) * 2 ** (6 - bit)
    return total


def wrap(turns):
    return turns - jnp.round(turns)


def encode(turns):
    return jnp.exp2(turns * SCALE)


def decode(code):
    return jnp.log2(code.astype(F32)) * (1.0 / SCALE)


def poly(coefs, square):
    value = jnp.full_like(square, coefs[-1])
    for c in coefs[-2::-1]:
        value = value * square + c
    return value


def tables(turns):
    square = turns * turns
    sine, cosine = poly(SIN, square) * turns, poly(COS, square)
    first = lax.broadcasted_iota(jnp.int32, turns.shape, 1) < 64
    sine_r, cosine_r = pltpu.roll(sine, 64, 1), pltpu.roll(cosine, 64, 1)
    return (
        (jnp.where(first, cosine, cosine_r), jnp.where(first, -sine, sine_r)),
        (jnp.where(first, cosine_r, cosine), jnp.where(first, -sine_r, sine)),
    )


def kernel(
    coef_hbm, interp_hbm, phase_hbm, out_ref,
    xin, phin, win, weights, a_cos, a_sin, stage, theirs,
    ph_send, ph_recv, co_send, co_recv, f_cos, f_sin, e_cos, e_sin, xs_even, xs_odd, xs_last,
    in_sem, ph_ssem, ph_rsem, co_ssem, co_rsem,
):
    hi, lo = lax.axis_index("hi"), lax.axis_index("lo")
    me = hi * LOWER + lo
    my_slot = reverse7(me)

    def place(d):
        return (lax.div(d, LOWER), lax.rem(d, LOWER))

    def others(f):
        def step(k, carry):
            f(lax.rem(me + k, DEVICES))
            return carry

        lax.fori_loop(1, DEVICES, step, 0, unroll=4)

    barrier = pltpu.get_barrier_semaphore()
    others(
        lambda d: pl.semaphore_signal(barrier, inc=1, device_id=place(d), device_id_type=MESH)
    )
    loads = [
        pltpu.make_async_copy(src, dst, in_sem.at[i])
        for i, (src, dst) in enumerate(((phase_hbm, phin), (coef_hbm, xin), (interp_hbm, win)))
    ]
    for load in loads:
        load.start()
    loads[0].wait()

    def angle(l, kind):
        rows = slice(64 * kind, 64 * kind + 64)
        halves = [phin[l, rows, 128 * q : 128 * q + 128] for q in range(2)]
        return jnp.concatenate(halves, axis=0) * 0.15915494309189535

    def put(group, row, turns):
        stage[group, pl.ds(row, 128, stride=8), :] = encode(turns.T)

    first = angle(0, 0)
    pairs = tables(first.T)
    for q in range(2):
        a_cos[q], a_sin[q] = pairs[q]
    put(1, 0, -first)
    put(1, 7, jnp.zeros_like(first))
    for l in range(LEVELS):
        after = angle(l, 2)
        if l < 7:
            put(0, l, angle(l, 1))
            put(2, l, wrap(after + angle(l + 1, 0)))
        else:
            put(2, 7, after)
        if l < 6:
            put(1, l + 1, after)
        elif l == 6:
            swapped = jnp.concatenate([after[64:128], after[0:64]], axis=0)
            put(0, 7, wrap(swapped + angle(7, 1)))

    def pack(j, carry):
        d = reverse7(j)
        for group in range(GROUPS):
            ph_send[group, d] = stage[group, pl.ds(8 * j, 8), :].astype(BF16)
        return carry

    lax.fori_loop(0, 128, pack, 0, unroll=4)

    pl.semaphore_wait(barrier, DEVICES - 1)

    def send(source, target, which, send_sem, recv_sem):
        others(
            lambda d: pltpu.make_async_remote_copy(
                src_ref=source.at[which, d], dst_ref=target.at[which, my_slot],
                send_sem=send_sem.at[which], recv_sem=recv_sem.at[which],
                device_id=place(d), device_id_type=MESH,
            ).start()
        )
        target[which, my_slot] = source[which, me]

    def wait_for(source, target, which, sem):
        rows = pl.ds(0, DEVICES - 1)
        pltpu.make_async_copy(source.at[which, rows], target.at[which, rows], sem.at[which]).wait()

    for group in (1, 0, 2):
        send(ph_send, ph_recv, group, ph_ssem, ph_rsem)

    loads[1].wait()

    def turn(j, carry):
        d = reverse7(j)
        for q in range(2):
            x = xin[q * 128 + j].astype(F32)
            cosine = jnp.broadcast_to(a_cos[q, pl.ds(j, 1), :], x.shape)
            sine = jnp.broadcast_to(a_sin[q, pl.ds(j, 1), :], x.shape)
            y = (x * cosine + pltpu.roll(x, 64, 1) * sine).astype(BF16)
            for h in range(2):
                co_send[2 * h + q, d] = y[8 * h : 8 * h + 8]
        return carry

    lax.fori_loop(0, 128, turn, 0, unroll=4)
    for c in range(4):
        send(co_send, co_recv, c, co_ssem, co_rsem)

    loads[2].wait()
    for l in range(LEVELS):
        empty = jnp.zeros((64, 64), F32)
        for part in range(2):
            block = win[l, part].astype(F32)
            row = part * 128
            weights[l, row : row + 64, :] = jnp.concatenate(
                [block, empty, empty, block], axis=1
            ).astype(BF16)
            weights[l, row + 64 : row + 128, :] = jnp.concatenate(
                [empty, block, block, empty], axis=1
            ).astype(BF16)

    def keep(cos_ref, sin_ref, t, turns):
        pairs = tables(turns)
        rows = pl.ds(pl.multiple_of(8 * t, 8), 8)
        for q in range(2):
            cos_ref[q, rows, :], sin_ref[q, rows, :] = pairs[q]

    wait_for(ph_send, ph_recv, 1, ph_rsem)

    def decode_theirs(t, carry):
        theirs[t] = decode(ph_recv[1, t])
        return carry

    lax.fori_loop(0, 128, decode_theirs, 0, unroll=8)
    wait_for(ph_send, ph_recv, 0, ph_rsem)

    def cross_tables(block, carry):
        flipped = [
            block + 2**k * (1 - 2 * lax.rem(lax.div(block, 2**k), 2)) for k in range(4)
        ]
        row = lax.broadcasted_iota(jnp.int32, (8, 128), 0)
        for i in range(8):
            t = 8 * block + i
            added = jnp.zeros((8, 128), F32)
            for l in range(7):
                partner = 8 * block + (i ^ 2**l) if l < 3 else 8 * flipped[l - 3] + i
                added = jnp.where(row == l, theirs[partner], added)
            keep(f_cos, f_sin, t, wrap(decode(ph_recv[0, t]) + added))
        return carry

    lax.fori_loop(0, 16, cross_tables, 0)
    wait_for(ph_send, ph_recv, 2, ph_rsem)

    def own_tables(t, carry):
        keep(e_cos, e_sin, t, decode(ph_recv[2, t]))
        return carry

    lax.fori_loop(0, 128, own_tables, 0, unroll=8)

    def lookup(cos_ref, sin_ref, q, t, index):
        row = pl.ds(8 * t + index, 1)
        return (
            jnp.broadcast_to(cos_ref[q, row, :], (8, 128)),
            jnp.broadcast_to(sin_ref[q, row, :], (8, 128)),
        )

    def own_angle(q, t, l):
        return lookup(e_cos, e_sin, q, t, l - 1)

    def cross_angle(q, t, l):
        return lookup(f_cos, f_sin, q, t, l)

    def turned(planes, angle):
        return planes[0] * angle[0] + planes[1] * angle[1]

    own, cross = slice(0, 128), slice(128, 256)

    def join(values):
        return jnp.concatenate(values, axis=0).astype(BF16)

    def multiply(source, l, use):
        for block in range(8):
            rows = slice(128 * block, 128 * block + 128)
            mixed = jnp.dot(source[rows, :], weights[l], preferred_element_type=F32)
            for i in range(8):
                use(8 * block + i, [
                    (mixed[r : r + 8, 0:128], mixed[r : r + 8, 128:256])
                    for r in (16 * i, 16 * i + 8)
                ])

    def levels(h, q):
        c = 2 * h + q
        wait_for(co_send, co_recv, c, co_rsem)
        buffers = (xs_even, xs_odd)

        def first_level(unit, carry):
            t = 2 * unit
            rows = pl.ds(pl.multiple_of(unit * 16, 16), 16)
            y = [co_recv[c, t + i] for i in range(2)]
            xs_even[rows, own] = jnp.concatenate(y, axis=0)
            planes = [(v.astype(F32), pltpu.roll(v.astype(F32), 64, 1)) for v in y]
            xs_even[rows, cross] = join(
                [turned(planes[1 - i], cross_angle(q, t + i, 0)) for i in range(2)]
            )
            return carry

        lax.fori_loop(0, 64, first_level, 0, unroll=8)
        for l in range(7):

            def use(unit, planes, l=l):
                other = unit if l == 6 else unit ^ 2**l
                rows = slice(16 * unit, 16 * unit + 16)
                far = slice(16 * other, 16 * other + 16)
                q_far = 1 - q if l == 6 else q
                mine = join(
                    [turned(planes[i], own_angle(q, 2 * unit + i, l + 1)) for i in range(2)]
                )
                given = join(
                    [turned(planes[i], cross_angle(q_far, 2 * other + i, l + 1)) for i in range(2)]
                )
                if l == 6:
                    xs_last[q, rows, own] = mine
                    xs_last[1 - q, far, cross] = given
                else:
                    buffers[(l + 1) % 2][rows, own] = mine
                    buffers[(l + 1) % 2][far, cross] = given

            multiply(buffers[l % 2], l, use)

    def half(h, carry):
        def part(q, carry):
            levels(h, q)
            return carry

        lax.fori_loop(0, 2, part, 0)

        def last(q, carry):
            def use(unit, planes):
                for i in range(2):
                    t = 2 * unit + i
                    out_ref[q * 128 + t, pl.ds(pl.multiple_of(8 * h, 8), 8), :] = turned(
                        planes[i], own_angle(q, t, 8)
                    ).astype(BF16)

            multiply(xs_last.at[q], 7, use)
            return carry

        lax.fori_loop(0, 2, last, 0)
        return carry

    lax.fori_loop(0, 2, half, 0)

    for group in range(GROUPS):
        wait_for(ph_send, ph_recv, group, ph_ssem)
    for c in range(4):
        wait_for(co_send, co_recv, c, co_ssem)


def body(coefficients, interpolation, phases):
    vmem, dma = pltpu.VMEM, pltpu.SemaphoreType.DMA
    return pl.pallas_call(
        kernel,
        out_shape=jax.ShapeDtypeStruct(coefficients.shape, BF16),
        in_specs=[pl.BlockSpec(memory_space=pltpu.HBM)] * 3,
        out_specs=pl.BlockSpec(memory_space=pltpu.VMEM),
        scratch_shapes=[
            vmem((256, 16, 128), BF16),
            vmem((LEVELS, 192, 256), F32),
            vmem((LEVELS, 2, 64, 64), BF16),
            vmem((LEVELS, 256, 256), BF16),
            vmem((2, 128, 128), F32),
            vmem((2, 128, 128), F32),
            vmem((GROUPS, 1024, 128), F32),
            vmem((128, 8, 128), F32),
            vmem((GROUPS, 128, 8, 128), BF16),
            vmem((GROUPS, 128, 8, 128), BF16),
            vmem((4, 128, 8, 128), BF16),
            vmem((4, 128, 8, 128), BF16),
            vmem((2, 1024, 128), F32),
            vmem((2, 1024, 128), F32),
            vmem((2, 1024, 128), F32),
            vmem((2, 1024, 128), F32),
            vmem((1024, 256), BF16),
            vmem((1024, 256), BF16),
            vmem((2, 1024, 256), BF16),
            dma((3,)),
            dma((GROUPS,)),
            dma((GROUPS,)),
            dma((4,)),
            dma((4,)),
        ],
        compiler_params=pltpu.CompilerParams(
            collective_id=0, has_side_effects=True, vmem_limit_bytes=209 * 2**18
        ),
    )(coefficients, interpolation, jnp.swapaxes(phases, 1, 2))


def solution(mesh):
    placed = (P(("hi", "lo"), None, None), P(), P(None, ("hi", "lo"), None))
    return jax.shard_map(
        body, mesh=mesh, in_specs=placed, out_specs=P(("hi", "lo"), None, None), check_vma=False
    )
```

time: 64 us -> 41.5 us (0.65); the launches traced: 63 us -> 41.4 us
  Pallas kernels: 60.1 us -> 39.4 us
  local copies, waits for them, and re-layouts: 2.91 us -> 1.92 us
    pallas_call x1, Pallas kernels: 60.1 us -> 39.4 us  [body(): pl.pallas_call(kernel, out_shape=jax.ShapeDtypeStruct(coefficients.shape,...]
    unnamed x6 -> x3, local copies, waits for them, and re-layouts: 2.91 us -> 1.92 us
where the time goes in v1:
time: 41.5 us; the launch traced here: 41.4 us
  Pallas kernels  39.4 us (95%)
  local copies, waits for them, and re-layouts  1.92 us (5%)
    pallas_call x1, Pallas kernels, body(): pl.pallas_call(kernel, out_shape=jax.ShapeDtypeStruct(coefficients.shape,...  39.4 us
    unnamed x3, local copies, waits for them, and re-layouts  1.92 us

profile of v1, /device:TPU:1, one launch (start us, length us, event | category | flops | bytes accessed | tf_op | source)
XLA Modules:
  0.0 41.4 jit_solution(16280669679990678183)
XLA Ops:
  0.0 0.0 copy-start
  0.0 0.9 %copy-done = bf16[8,2,64,64]{3,2,1,0:T(8,128)(2,1)S(1)} copy-done((bf16[8,2,64,64]{3,2,1,0:T(8,128)(2,1)S(1)}, bf16[8,2,64,64]{3,2,1,0:T(8,128)(2,1)}, u32[]{:S(2)}) %copy-start) | copy-done | bytes 131096
  1.0 39.4 %shard_map.37 = bf16[256,16,128]{2,1,0:T(8,128)(2,1)S(1)} custom-call(bf16[256,16,128]{2,1,0:T(8,128)(2,1)} %coef_hbm.1, bf16[8,2,64,64]{3,2,1,0:T(8,128)(2,1)S(1)} %copy-done, f32[8,192,256]{2,1,0:T(8,128)} %bitcast.1), custom_call_target="tpu_custom_call" | custom-call | tf_op jit(solution)/shard_map/pallas_call | solution.py:314
  40.4 1.0 %copy.5 = bf16[256,16,128]{2,1,0:T(8,128)(2,1)} copy(bf16[256,16,128]{2,1,0:T(8,128)(2,1)S(1)} %shard_map.37) | data formatting | bytes 2097152
Async XLA Ops:
  0.0 0.9 %copy-start = (bf16[8,2,64,64]{3,2,1,0:T(8,128)(2,1)S(1)}, bf16[8,2,64,64]{3,2,1,0:T(8,128)(2,1)}, u32[]{:S(2)}) copy-start(bf16[8,2,64,64]{3,2,1,0:T(8,128)(2,1)} %interp_hbm.1) | copy-start | bytes 393220

commit v2 on v1

--- a/solution.py
+++ b/solution.py
@@ -19,11 +19,25 @@
 COS = (0.999999216, -19.7389812, 64.9286774, -85.2717657, 58.7907877, -21.0709971)
 
 
-def reverse7(i):
+def reverse(i, bits):
     total = 0
-    for bit in range(7):
-        total = total + lax.rem(lax.div(i, 2**bit), 2) * 2 ** (6 - bit)
+    for bit in range(bits):
+        total = total + lax.rem(lax.div(i, 2**bit), 2) * 2 ** (bits - 1 - bit)
     return total
+
+
+def each_destination(f):
+    def step(upper, carry):
+        tail = reverse(upper, 4)
+        for lower in range(8):
+            f(8 * upper + lower, 16 * reverse_static(lower) + tail)
+        return carry
+
+    lax.fori_loop(0, 16, step, 0)
+
+
+def reverse_static(i):
+    return (i % 2) * 4 + (i // 2 % 2) * 2 + i // 4
 
 
 def wrap(turns):
@@ -64,7 +78,7 @@
 ):
     hi, lo = lax.axis_index("hi"), lax.axis_index("lo")
     me = hi * LOWER + lo
-    my_slot = reverse7(me)
+    my_slot = reverse(me, 7)
 
     def place(d):
         return (lax.div(d, LOWER), lax.rem(d, LOWER))
@@ -96,34 +110,30 @@
     def put(group, row, turns):
         stage[group, pl.ds(row, 128, stride=8), :] = encode(turns.T)
 
-    first = angle(0, 0)
-    pairs = tables(first.T)
-    for q in range(2):
-        a_cos[q], a_sin[q] = pairs[q]
-    put(1, 0, -first)
-    put(1, 7, jnp.zeros_like(first))
-    for l in range(LEVELS):
-        after = angle(l, 2)
-        if l < 7:
-            put(0, l, angle(l, 1))
-            put(2, l, wrap(after + angle(l + 1, 0)))
+    def pack(group):
+        def step(j, d):
+            rows = pl.ds(pl.multiple_of(8 * j, 8), 8)
+            ph_send[group, d] = stage[group, rows, :].astype(BF16)
+
+        each_destination(step)
+
+    def prepare(group):
+        if group == 0:
+            for l in range(7):
+                put(0, l, angle(l, 1))
+            theirs7 = angle(6, 2)
+            swapped = jnp.concatenate([theirs7[64:128], theirs7[0:64]], axis=0)
+            put(0, 7, wrap(swapped + angle(7, 1)))
+        elif group == 1:
+            put(1, 0, -angle(0, 0))
+            for l in range(6):
+                put(1, l + 1, angle(l, 2))
+            put(1, 7, jnp.zeros((128, 128), F32))
         else:
-            put(2, 7, after)
-        if l < 6:
-            put(1, l + 1, after)
-        elif l == 6:
-            swapped = jnp.concatenate([after[64:128], after[0:64]], axis=0)
-            put(0, 7, wrap(swapped + angle(7, 1)))
-
-    def pack(j, carry):
-        d = reverse7(j)
-        for group in range(GROUPS):
-            ph_send[group, d] = stage[group, pl.ds(8 * j, 8), :].astype(BF16)
-        return carry
-
-    lax.fori_loop(0, 128, pack, 0, unroll=4)
-
-    pl.semaphore_wait(barrier, DEVICES - 1)
+            for l in range(7):
+                put(2, l, wrap(angle(l, 2) + angle(l + 1, 0)))
+            put(2, 7, angle(7, 2))
+        pack(group)
 
     def send(source, target, which, send_sem, recv_sem):
         others(
@@ -139,13 +149,20 @@
         rows = pl.ds(0, DEVICES - 1)
         pltpu.make_async_copy(source.at[which, rows], target.at[which, rows], sem.at[which]).wait()
 
-    for group in (1, 0, 2):
-        send(ph_send, ph_recv, group, ph_ssem, ph_rsem)
+    prepare(1)
+    pl.semaphore_wait(barrier, DEVICES - 1)
+    send(ph_send, ph_recv, 1, ph_ssem, ph_rsem)
+    prepare(0)
+    send(ph_send, ph_recv, 0, ph_ssem, ph_rsem)
+    prepare(2)
+    send(ph_send, ph_recv, 2, ph_ssem, ph_rsem)
+    pairs = tables(angle(0, 0).T)
+    for q in range(2):
+        a_cos[q], a_sin[q] = pairs[q]
 
     loads[1].wait()
 
-    def turn(j, carry):
-        d = reverse7(j)
+    def turn(j, d):
         for q in range(2):
             x = xin[q * 128 + j].astype(F32)
             cosine = jnp.broadcast_to(a_cos[q, pl.ds(j, 1), :], x.shape)
@@ -153,9 +170,8 @@
             y = (x * cosine + pltpu.roll(x, 64, 1) * sine).astype(BF16)
             for h in range(2):
                 co_send[2 * h + q, d] = y[8 * h : 8 * h + 8]
-        return carry
-
-    lax.fori_loop(0, 128, turn, 0, unroll=4)
+
+    each_destination(turn)
     for c in range(4):
         send(co_send, co_recv, c, co_ssem, co_rsem)
 
@@ -232,11 +248,11 @@
         return jnp.concatenate(values, axis=0).astype(BF16)
 
     def multiply(source, l, use):
-        for block in range(8):
-            rows = slice(128 * block, 128 * block + 128)
+        for block in range(2):
+            rows = slice(512 * block, 512 * block + 512)
             mixed = jnp.dot(source[rows, :], weights[l], preferred_element_type=F32)
-            for i in range(8):
-                use(8 * block + i, [
+            for i in range(32):
+                use(32 * block + i, [
                     (mixed[r : r + 8, 0:128], mixed[r : r + 8, 128:256])
                     for r in (16 * i, 16 * i + 8)
                 ])

time: 41.5 us -> 38.6 us (0.930)
  Pallas kernels: 39.4 us -> 36.5 us
    pallas_call x1, Pallas kernels: 39.4 us -> 36.5 us  [body(): pl.pallas_call(kernel, out_shape=jax.ShapeDtypeStruct(coefficients.shape,...]
where the time goes in v2:
time: 38.6 us; the launch traced here: 38.4 us
  Pallas kernels  36.5 us (95%)
  local copies, waits for them, and re-layouts  1.92 us (5%)
    pallas_call x1, Pallas kernels, body(): pl.pallas_call(kernel, out_shape=jax.ShapeDtypeStruct(coefficients.shape,...  36.5 us
    unnamed x3, local copies, waits for them, and re-layouts  1.92 us

profile of v2, /device:TPU:1, one launch (start us, length us, event | category | flops | bytes accessed | tf_op | source)
XLA Modules:
  0.0 38.4 jit_solution(15153135776850770507)
XLA Ops:
  0.0 0.0 copy-start
  0.0 0.9 %copy-done = bf16[8,2,64,64]{3,2,1,0:T(8,128)(2,1)S(1)} copy-done((bf16[8,2,64,64]{3,2,1,0:T(8,128)(2,1)S(1)}, bf16[8,2,64,64]{3,2,1,0:T(8,128)(2,1)}, u32[]{:S(2)}) %copy-start) | copy-done | bytes 131096
  1.0 36.5 %shard_map.37 = bf16[256,16,128]{2,1,0:T(8,128)(2,1)S(1)} custom-call(bf16[256,16,128]{2,1,0:T(8,128)(2,1)} %coef_hbm.1, bf16[8,2,64,64]{3,2,1,0:T(8,128)(2,1)S(1)} %copy-done, f32[8,192,256]{2,1,0:T(8,128)} %bitcast.1), custom_call_target="tpu_custom_call" | custom-call | tf_op jit(solution)/shard_map/pallas_call | solution.py:330
  37.5 1.0 %copy.5 = bf16[256,16,128]{2,1,0:T(8,128)(2,1)} copy(bf16[256,16,128]{2,1,0:T(8,128)(2,1)S(1)} %shard_map.37) | data formatting | bytes 2097152
Async XLA Ops:
  0.0 0.9 %copy-start = (bf16[8,2,64,64]{3,2,1,0:T(8,128)(2,1)S(1)}, bf16[8,2,64,64]{3,2,1,0:T(8,128)(2,1)}, u32[]{:S(2)}) copy-start(bf16[8,2,64,64]{3,2,1,0:T(8,128)(2,1)} %interp_hbm.1) | copy-start | bytes 393220

commit v3 on v2

--- a/solution.py
+++ b/solution.py
@@ -12,6 +12,7 @@
 DEVICES = 128
 LOWER = 32
 LEVELS = 8
+UNITS = 16
 GROUPS = 3
 SCALE = 240.0
 
@@ -247,15 +248,22 @@
     def join(values):
         return jnp.concatenate(values, axis=0).astype(BF16)
 
-    def multiply(source, l, use):
-        for block in range(2):
-            rows = slice(512 * block, 512 * block + 512)
-            mixed = jnp.dot(source[rows, :], weights[l], preferred_element_type=F32)
-            for i in range(32):
-                use(32 * block + i, [
+    def pipeline(tasks):
+        def consume(block, use, mixed):
+            for i in range(UNITS):
+                use(UNITS * block + i, [
                     (mixed[r : r + 8, 0:128], mixed[r : r + 8, 128:256])
                     for r in (16 * i, 16 * i + 8)
                 ])
+
+        waiting = None
+        for source, l, block, use in tasks:
+            rows = slice(16 * UNITS * block, 16 * UNITS * (block + 1))
+            mixed = jnp.dot(source[rows, :], weights[l], preferred_element_type=F32)
+            if waiting is not None:
+                consume(*waiting)
+            waiting = (block, use, mixed)
+        consume(*waiting)
 
     def levels(h, q):
         c = 2 * h + q
@@ -274,6 +282,7 @@
             return carry
 
         lax.fori_loop(0, 64, first_level, 0, unroll=8)
+        tasks = []
         for l in range(7):
 
             def use(unit, planes, l=l):
@@ -294,7 +303,8 @@
                     buffers[(l + 1) % 2][rows, own] = mine
                     buffers[(l + 1) % 2][far, cross] = given
 
-            multiply(buffers[l % 2], l, use)
+            tasks += [(buffers[l % 2], l, block, use) for block in range(64 // UNITS)]
+        pipeline(tasks)
 
     def half(h, carry):
         def part(q, carry):
@@ -303,18 +313,18 @@
 
         lax.fori_loop(0, 2, part, 0)
 
-        def last(q, carry):
-            def use(unit, planes):
+        tasks = []
+        for q in range(2):
+
+            def use(unit, planes, q=q):
                 for i in range(2):
                     t = 2 * unit + i
                     out_ref[q * 128 + t, pl.ds(pl.multiple_of(8 * h, 8), 8), :] = turned(
                         planes[i], own_angle(q, t, 8)
                     ).astype(BF16)
 
-            multiply(xs_last.at[q], 7, use)
-            return carry
-
-        lax.fori_loop(0, 2, last, 0)
+            tasks += [(xs_last.at[q], 7, block, use) for block in range(64 // UNITS)]
+        pipeline(tasks)
         return carry
 
     lax.fori_loop(0, 2, half, 0)
@@ -327,6 +337,10 @@
 
 def body(coefficients, interpolation, phases):
     vmem, dma = pltpu.VMEM, pltpu.SemaphoreType.DMA
+    operands = [
+        pltpu.with_memory_space_constraint(x, pltpu.HBM)
+        for x in (coefficients, interpolation, jnp.swapaxes(phases, 1, 2))
+    ]
     return pl.pallas_call(
         kernel,
         out_shape=jax.ShapeDtypeStruct(coefficients.shape, BF16),
@@ -359,9 +373,9 @@
             dma((4,)),
         ],
         compiler_params=pltpu.CompilerParams(
-            collective_id=0, has_side_effects=True, vmem_limit_bytes=209 * 2**18
+            collective_id=0, has_side_effects=True, vmem_limit_bytes=48 * 2**20
         ),
-    )(coefficients, interpolation, jnp.swapaxes(phases, 1, 2))
+    )(*operands)
 
 
 def solution(mesh):

time: 38.6 us -> 37.6 us (0.974)
  local copies, waits for them, and re-layouts: 1.92 us -> 0.97 us
    unnamed x3 -> x1, local copies, waits for them, and re-layouts: 1.92 us -> 0.97 us
where the time goes in v3:
time: 37.6 us; the launch traced here: 37.4 us
  Pallas kernels  36.5 us (97%)
  local copies, waits for them, and re-layouts  0.97 us (3%)
    pallas_call x1, Pallas kernels, body(): pl.pallas_call(kernel, out_shape=jax.ShapeDtypeStruct(coefficients.shape,...  36.5 us
    unnamed x1, local copies, waits for them, and re-layouts  0.97 us

profile of v3, /device:TPU:1, one launch (start us, length us, event | category | flops | bytes accessed | tf_op | source)
XLA Modules:
  0.0 37.4 jit_solution(11613043616061117438)
XLA Ops:
  0.0 36.5 %shard_map.37 = bf16[256,16,128]{2,1,0:T(8,128)(2,1)S(1)} custom-call(bf16[256,16,128]{2,1,0:T(8,128)(2,1)} %coef_hbm.1, bf16[8,2,64,64]{3,2,1,0:T(8,128)(2,1)} %interp_hbm.1, f32[8,192,256]{2,1,0:T(8,128)} %bitcast.1), custom_call_target="tpu_custom_call" | custom-call | tf_op jit(solution)/shard_map/pallas_call | solution.py:344
  36.5 1.0 %copy.5 = bf16[256,16,128]{2,1,0:T(8,128)(2,1)} copy(bf16[256,16,128]{2,1,0:T(8,128)(2,1)S(1)} %shard_map.37) | data formatting | bytes 2097152

commit v4 on v3

--- a/solution.py
+++ b/solution.py
@@ -13,7 +13,7 @@
 LOWER = 32
 LEVELS = 8
 UNITS = 16
-GROUPS = 3
+GROUPS = 2
 SCALE = 240.0
 
 SIN = (6.28305505, -41.3311661, 81.3660033, -74.4730454, 32.7714685)
@@ -73,9 +73,9 @@
 
 def kernel(
     coef_hbm, interp_hbm, phase_hbm, out_ref,
-    xin, phin, win, weights, a_cos, a_sin, stage, theirs,
+    xin, phin, win, weights, a_cos, a_sin, stage, ex_send, ex_recv,
     ph_send, ph_recv, co_send, co_recv, f_cos, f_sin, e_cos, e_sin, xs_even, xs_odd, xs_last,
-    in_sem, ph_ssem, ph_rsem, co_ssem, co_rsem,
+    in_sem, ex_ssem, ex_rsem, ph_ssem, ph_rsem, co_ssem, co_rsem,
 ):
     hi, lo = lax.axis_index("hi"), lax.axis_index("lo")
     me = hi * LOWER + lo
@@ -84,12 +84,12 @@
     def place(d):
         return (lax.div(d, LOWER), lax.rem(d, LOWER))
 
-    def others(f):
+    def others(f, first=1, end=DEVICES):
         def step(k, carry):
             f(lax.rem(me + k, DEVICES))
             return carry
 
-        lax.fori_loop(1, DEVICES, step, 0, unroll=4)
+        lax.fori_loop(first, end, step, 0, unroll=4)
 
     barrier = pltpu.get_barrier_semaphore()
     others(
@@ -118,45 +118,44 @@
 
         each_destination(step)
 
-    def prepare(group):
-        if group == 0:
-            for l in range(7):
-                put(0, l, angle(l, 1))
-            theirs7 = angle(6, 2)
-            swapped = jnp.concatenate([theirs7[64:128], theirs7[0:64]], axis=0)
-            put(0, 7, wrap(swapped + angle(7, 1)))
-        elif group == 1:
-            put(1, 0, -angle(0, 0))
-            for l in range(6):
-                put(1, l + 1, angle(l, 2))
-            put(1, 7, jnp.zeros((128, 128), F32))
-        else:
-            for l in range(7):
-                put(2, l, wrap(angle(l, 2) + angle(l + 1, 0)))
-            put(2, 7, angle(7, 2))
-        pack(group)
-
-    def send(source, target, which, send_sem, recv_sem):
+    ex_send[0] = encode(-angle(0, 0)).astype(BF16)
+    for l in range(1, 7):
+        ex_send[l] = encode(angle(l - 1, 2)).astype(BF16)
+    for l in range(7):
+        put(1, l, wrap(angle(l, 2) + angle(l + 1, 0)))
+    put(1, 7, angle(7, 2))
+    pack(1)
+
+    def send(source, target, which, send_sem, recv_sem, first=1, end=DEVICES):
         others(
             lambda d: pltpu.make_async_remote_copy(
                 src_ref=source.at[which, d], dst_ref=target.at[which, my_slot],
                 send_sem=send_sem.at[which], recv_sem=recv_sem.at[which],
                 device_id=place(d), device_id_type=MESH,
-            ).start()
+            ).start(),
+            first, end,
         )
-        target[which, my_slot] = source[which, me]
+        if first == 1:
+            target[which, my_slot] = source[which, me]
 
     def wait_for(source, target, which, sem):
         rows = pl.ds(0, DEVICES - 1)
         pltpu.make_async_copy(source.at[which, rows], target.at[which, rows], sem.at[which]).wait()
 
-    prepare(1)
     pl.semaphore_wait(barrier, DEVICES - 1)
+    exchanges = []
+    for l in range(7):
+        bit = 2 ** (6 - l)
+        partner = me + bit * (1 - 2 * lax.rem(lax.div(me, bit), 2))
+        exchanges.append(
+            pltpu.make_async_remote_copy(
+                src_ref=ex_send.at[l], dst_ref=ex_recv.at[l],
+                send_sem=ex_ssem.at[l], recv_sem=ex_rsem.at[l],
+                device_id=place(partner), device_id_type=MESH,
+            )
+        )
+        exchanges[-1].start()
     send(ph_send, ph_recv, 1, ph_ssem, ph_rsem)
-    prepare(0)
-    send(ph_send, ph_recv, 0, ph_ssem, ph_rsem)
-    prepare(2)
-    send(ph_send, ph_recv, 2, ph_ssem, ph_rsem)
     pairs = tables(angle(0, 0).T)
     for q in range(2):
         a_cos[q], a_sin[q] = pairs[q]
@@ -173,7 +172,18 @@
                 co_send[2 * h + q, d] = y[8 * h : 8 * h + 8]
 
     each_destination(turn)
-    for c in range(4):
+    send(co_send, co_recv, 0, co_ssem, co_rsem, 1, 64)
+
+    for l in range(7):
+        exchanges[l].wait_recv()
+        put(0, l, wrap(angle(l, 1) + decode(ex_recv[l])))
+    theirs = angle(6, 2)
+    swapped = jnp.concatenate([theirs[64:128], theirs[0:64]], axis=0)
+    put(0, 7, wrap(swapped + angle(7, 1)))
+    pack(0)
+    send(ph_send, ph_recv, 0, ph_ssem, ph_rsem)
+    send(co_send, co_recv, 0, co_ssem, co_rsem, 64, DEVICES)
+    for c in range(1, 4):
         send(co_send, co_recv, c, co_ssem, co_rsem)
 
     loads[2].wait()
@@ -195,37 +205,14 @@
         for q in range(2):
             cos_ref[q, rows, :], sin_ref[q, rows, :] = pairs[q]
 
-    wait_for(ph_send, ph_recv, 1, ph_rsem)
-
-    def decode_theirs(t, carry):
-        theirs[t] = decode(ph_recv[1, t])
-        return carry
-
-    lax.fori_loop(0, 128, decode_theirs, 0, unroll=8)
-    wait_for(ph_send, ph_recv, 0, ph_rsem)
-
-    def cross_tables(block, carry):
-        flipped = [
-            block + 2**k * (1 - 2 * lax.rem(lax.div(block, 2**k), 2)) for k in range(4)
-        ]
-        row = lax.broadcasted_iota(jnp.int32, (8, 128), 0)
-        for i in range(8):
-            t = 8 * block + i
-            added = jnp.zeros((8, 128), F32)
-            for l in range(7):
-                partner = 8 * block + (i ^ 2**l) if l < 3 else 8 * flipped[l - 3] + i
-                added = jnp.where(row == l, theirs[partner], added)
-            keep(f_cos, f_sin, t, wrap(decode(ph_recv[0, t]) + added))
-        return carry
-
-    lax.fori_loop(0, 16, cross_tables, 0)
-    wait_for(ph_send, ph_recv, 2, ph_rsem)
-
-    def own_tables(t, carry):
-        keep(e_cos, e_sin, t, decode(ph_recv[2, t]))
-        return carry
-
-    lax.fori_loop(0, 128, own_tables, 0, unroll=8)
+    for group, cos_ref, sin_ref in ((1, e_cos, e_sin), (0, f_cos, f_sin)):
+        wait_for(ph_send, ph_recv, group, ph_rsem)
+
+        def one_slot(t, carry, group=group, cos_ref=cos_ref, sin_ref=sin_ref):
+            keep(cos_ref, sin_ref, t, decode(ph_recv[group, t]))
+            return carry
+
+        lax.fori_loop(0, 128, one_slot, 0, unroll=8)
 
     def lookup(cos_ref, sin_ref, q, t, index):
         row = pl.ds(8 * t + index, 1)
@@ -248,7 +235,7 @@
     def join(values):
         return jnp.concatenate(values, axis=0).astype(BF16)
 
-    def pipeline(tasks):
+    def pipeline(tasks, ahead=None):
         def consume(block, use, mixed):
             for i in range(UNITS):
                 use(UNITS * block + i, [
@@ -259,6 +246,8 @@
         waiting = None
         for source, l, block, use in tasks:
             rows = slice(16 * UNITS * block, 16 * UNITS * (block + 1))
+            if l == 0:
+                ahead(block)
             mixed = jnp.dot(source[rows, :], weights[l], preferred_element_type=F32)
             if waiting is not None:
                 consume(*waiting)
@@ -270,18 +259,17 @@
         wait_for(co_send, co_recv, c, co_rsem)
         buffers = (xs_even, xs_odd)
 
-        def first_level(unit, carry):
-            t = 2 * unit
-            rows = pl.ds(pl.multiple_of(unit * 16, 16), 16)
-            y = [co_recv[c, t + i] for i in range(2)]
-            xs_even[rows, own] = jnp.concatenate(y, axis=0)
-            planes = [(v.astype(F32), pltpu.roll(v.astype(F32), 64, 1)) for v in y]
-            xs_even[rows, cross] = join(
-                [turned(planes[1 - i], cross_angle(q, t + i, 0)) for i in range(2)]
-            )
-            return carry
-
-        lax.fori_loop(0, 64, first_level, 0, unroll=8)
+        def first_level(block):
+            for unit in range(UNITS * block, UNITS * (block + 1)):
+                t = 2 * unit
+                rows = slice(16 * unit, 16 * unit + 16)
+                y = [co_recv[c, t + i] for i in range(2)]
+                xs_even[rows, own] = jnp.concatenate(y, axis=0)
+                planes = [(v.astype(F32), pltpu.roll(v.astype(F32), 64, 1)) for v in y]
+                xs_even[rows, cross] = join(
+                    [turned(planes[1 - i], cross_angle(q, t + i, 0)) for i in range(2)]
+                )
+
         tasks = []
         for l in range(7):
 
@@ -304,7 +292,7 @@
                     buffers[(l + 1) % 2][far, cross] = given
 
             tasks += [(buffers[l % 2], l, block, use) for block in range(64 // UNITS)]
-        pipeline(tasks)
+        pipeline(tasks, first_level)
 
     def half(h, carry):
         def part(q, carry):
@@ -329,6 +317,8 @@
 
     lax.fori_loop(0, 2, half, 0)
 
+    for l in range(7):
+        exchanges[l].wait_send()
     for group in range(GROUPS):
         wait_for(ph_send, ph_recv, group, ph_ssem)
     for c in range(4):
@@ -354,7 +344,8 @@
             vmem((2, 128, 128), F32),
             vmem((2, 128, 128), F32),
             vmem((GROUPS, 1024, 128), F32),
-            vmem((128, 8, 128), F32),
+            vmem((7, 128, 128), BF16),
+            vmem((7, 128, 128), BF16),
             vmem((GROUPS, 128, 8, 128), BF16),
             vmem((GROUPS, 128, 8, 128), BF16),
             vmem((4, 128, 8, 128), BF16),
@@ -367,6 +358,8 @@
             vmem((1024, 256), BF16),
             vmem((2, 1024, 256), BF16),
             dma((3,)),
+            dma((7,)),
+            dma((7,)),
             dma((GROUPS,)),
             dma((GROUPS,)),
             dma((4,)),

time: 37.6 us -> 35.4 us (0.941)
  Pallas kernels: 36.5 us -> 34.2 us
    pallas_call x1, Pallas kernels: 36.5 us -> 34.2 us  [body(): pl.pallas_call(kernel, out_shape=jax.ShapeDtypeStruct(coefficients.shape,...]
where the time goes in v4:
time: 35.4 us; the launch traced here: 35.2 us
  Pallas kernels  34.2 us (97%)
  local copies, waits for them, and re-layouts  0.97 us (3%)
    pallas_call x1, Pallas kernels, body(): pl.pallas_call(kernel, out_shape=jax.ShapeDtypeStruct(coefficients.shape,...  34.2 us
    unnamed x1, local copies, waits for them, and re-layouts  0.97 us

profile of v4, /device:TPU:1, one launch (start us, length us, event | category | flops | bytes accessed | tf_op | source)
XLA Modules:
  0.0 35.2 jit_solution(15057235890270062081)
XLA Ops:
  0.0 34.2 %shard_map.37 = bf16[256,16,128]{2,1,0:T(8,128)(2,1)S(1)} custom-call(bf16[256,16,128]{2,1,0:T(8,128)(2,1)} %coef_hbm.1, bf16[8,2,64,64]{3,2,1,0:T(8,128)(2,1)} %interp_hbm.1, f32[8,192,256]{2,1,0:T(8,128)} %bitcast.1), custom_call_target="tpu_custom_call" | custom-call | tf_op jit(solution)/shard_map/pallas_call | solution.py:334
  34.2 1.0 %copy.5 = bf16[256,16,128]{2,1,0:T(8,128)(2,1)} copy(bf16[256,16,128]{2,1,0:T(8,128)(2,1)S(1)} %shard_map.37) | data formatting | bytes 2097152

commit v5 on v4

--- a/solution.py
+++ b/solution.py
@@ -1,4 +1,4 @@
-import functools
+import itertools
 
 import jax
 import jax.numpy as jnp
@@ -18,6 +18,10 @@
 
 SIN = (6.28305505, -41.3311661, 81.3660033, -74.4730454, 32.7714685)
 COS = (0.999999216, -19.7389812, 64.9286774, -85.2717657, 58.7907877, -21.0709971)
+
+FAR_FIRST = sorted(
+    itertools.product(range(4), repeat=3), key=lambda v: -sum(min(d, 4 - d) for d in v)
+)
 
 
 def reverse(i, bits):
@@ -92,9 +96,18 @@
         lax.fori_loop(first, end, step, 0, unroll=4)
 
     barrier = pltpu.get_barrier_semaphore()
-    others(
-        lambda d: pl.semaphore_signal(barrier, inc=1, device_id=place(d), device_id_type=MESH)
-    )
+    x = lax.rem(lax.div(lo, 4), 2) * 2 + lax.div(hi, 2)
+    at_x = [lax.rem(x + step, 4) for step in range(4)]
+    hi_x = [lax.rem(v, 2) * 2 for v in at_x]
+    lo_x = [lax.div(v, 2) * 4 for v in at_x]
+    lo_y = [lax.rem(lax.rem(lo, 4) + step, 4) for step in range(4)]
+    lo_z = [lax.rem(lax.div(lo, 8) + step, 4) * 8 for step in range(4)]
+    cores = [lax.rem(hi, 2), 1 - lax.rem(hi, 2)]
+    for dx, dy, dz in FAR_FIRST:
+        for dc in range(2):
+            if (dx, dy, dz, dc) != (0, 0, 0, 0):
+                target = (hi_x[dx] + cores[dc], lo_z[dz] + lo_x[dx] + lo_y[dy])
+                pl.semaphore_signal(barrier, inc=1, device_id=target, device_id_type=MESH)
     loads = [
         pltpu.make_async_copy(src, dst, in_sem.at[i])
         for i, (src, dst) in enumerate(((phase_hbm, phin), (coef_hbm, xin), (interp_hbm, win)))
@@ -121,10 +134,6 @@
     ex_send[0] = encode(-angle(0, 0)).astype(BF16)
     for l in range(1, 7):
         ex_send[l] = encode(angle(l - 1, 2)).astype(BF16)
-    for l in range(7):
-        put(1, l, wrap(angle(l, 2) + angle(l + 1, 0)))
-    put(1, 7, angle(7, 2))
-    pack(1)
 
     def send(source, target, which, send_sem, recv_sem, first=1, end=DEVICES):
         others(
@@ -155,6 +164,10 @@
             )
         )
         exchanges[-1].start()
+    for l in range(7):
+        put(1, l, wrap(angle(l, 2) + angle(l + 1, 0)))
+    put(1, 7, angle(7, 2))
+    pack(1)
     send(ph_send, ph_recv, 1, ph_ssem, ph_rsem)
     pairs = tables(angle(0, 0).T)
     for q in range(2):

time: 35.4 us -> 35.2 us (level)
  no operation moved by 1% of the time
where the time goes in v5:
time: 35.2 us; the launch traced here: 35 us
  Pallas kernels  34.1 us (97%)
  local copies, waits for them, and re-layouts  0.97 us (3%)
    pallas_call x1, Pallas kernels, body(): pl.pallas_call(kernel, out_shape=jax.ShapeDtypeStruct(coefficients.shape,...  34.1 us
    unnamed x1, local copies, waits for them, and re-layouts  0.97 us

profile of v5, /device:TPU:1, one launch (start us, length us, event | category | flops | bytes accessed | tf_op | source)
XLA Modules:
  0.0 35.0 jit_solution(6664052674517075550)
XLA Ops:
  0.0 34.1 %shard_map.37 = bf16[256,16,128]{2,1,0:T(8,128)(2,1)S(1)} custom-call(bf16[256,16,128]{2,1,0:T(8,128)(2,1)} %coef_hbm.1, bf16[8,2,64,64]{3,2,1,0:T(8,128)(2,1)} %interp_hbm.1, f32[8,192,256]{2,1,0:T(8,128)} %bitcast.1), custom_call_target="tpu_custom_call" | custom-call | tf_op jit(solution)/shard_map/pallas_call | solution.py:347
  34.1 1.0 %copy.5 = bf16[256,16,128]{2,1,0:T(8,128)(2,1)} copy(bf16[256,16,128]{2,1,0:T(8,128)(2,1)S(1)} %shard_map.37) | data formatting | bytes 2097152

commit v6 on v5

--- a/solution.py
+++ b/solution.py
@@ -19,6 +19,7 @@
 SIN = (6.28305505, -41.3311661, 81.3660033, -74.4730454, 32.7714685)
 COS = (0.999999216, -19.7389812, 64.9286774, -85.2717657, 58.7907877, -21.0709971)
 
+FAR_LEVELS_FIRST = (2, 4, 5, 0, 3, 6, 1)
 FAR_FIRST = sorted(
     itertools.product(range(4), repeat=3), key=lambda v: -sum(min(d, 4 - d) for d in v)
 )
@@ -152,18 +153,16 @@
         pltpu.make_async_copy(source.at[which, rows], target.at[which, rows], sem.at[which]).wait()
 
     pl.semaphore_wait(barrier, DEVICES - 1)
-    exchanges = []
-    for l in range(7):
+    exchanges = {}
+    for l in FAR_LEVELS_FIRST:
         bit = 2 ** (6 - l)
         partner = me + bit * (1 - 2 * lax.rem(lax.div(me, bit), 2))
-        exchanges.append(
-            pltpu.make_async_remote_copy(
-                src_ref=ex_send.at[l], dst_ref=ex_recv.at[l],
-                send_sem=ex_ssem.at[l], recv_sem=ex_rsem.at[l],
-                device_id=place(partner), device_id_type=MESH,
-            )
+        exchanges[l] = pltpu.make_async_remote_copy(
+            src_ref=ex_send.at[l], dst_ref=ex_recv.at[l],
+            send_sem=ex_ssem.at[l], recv_sem=ex_rsem.at[l],
+            device_id=place(partner), device_id_type=MESH,
         )
-        exchanges[-1].start()
+        exchanges[l].start()
     for l in range(7):
         put(1, l, wrap(angle(l, 2) + angle(l + 1, 0)))
     put(1, 7, angle(7, 2))
@@ -187,7 +186,7 @@
     each_destination(turn)
     send(co_send, co_recv, 0, co_ssem, co_rsem, 1, 64)
 
-    for l in range(7):
+    for l in reversed(FAR_LEVELS_FIRST):
         exchanges[l].wait_recv()
         put(0, l, wrap(angle(l, 1) + decode(ex_recv[l])))
     theirs = angle(6, 2)

time: 35.2 us -> 35.3 us (level)
  no operation moved by 1% of the time
where the time goes in v6:
time: 35.3 us; the launch traced here: 35.2 us
  Pallas kernels  34.2 us (97%)
  local copies, waits for them, and re-layouts  0.97 us (3%)
    pallas_call x1, Pallas kernels, body(): pl.pallas_call(kernel, out_shape=jax.ShapeDtypeStruct(coefficients.shape,...  34.2 us
    unnamed x1, local copies, waits for them, and re-layouts  0.97 us

profile of v6, /device:TPU:1, one launch (start us, length us, event | category | flops | bytes accessed | tf_op | source)
XLA Modules:
  0.0 35.2 jit_solution(15317851965096044850)
XLA Ops:
  0.0 34.2 %shard_map.37 = bf16[256,16,128]{2,1,0:T(8,128)(2,1)S(1)} custom-call(bf16[256,16,128]{2,1,0:T(8,128)(2,1)} %coef_hbm.1, bf16[8,2,64,64]{3,2,1,0:T(8,128)(2,1)} %interp_hbm.1, f32[8,192,256]{2,1,0:T(8,128)} %bitcast.1), custom_call_target="tpu_custom_call" | custom-call | tf_op jit(solution)/shard_map/pallas_call | solution.py:346
  34.2 1.0 %copy.5 = bf16[256,16,128]{2,1,0:T(8,128)(2,1)} copy(bf16[256,16,128]{2,1,0:T(8,128)(2,1)S(1)} %shard_map.37) | data formatting | bytes 2097152
